TPU v7x, 256 devices: a whole 4x4x8 slice. The times are simulated.
256 devices in a mesh: freq: 4 (over y_hi, core), blk: 64 (over x, y_lo, z).
Axes of the slice: x: 4, y: 4 (y_hi: 2, y_lo: 2; y = y_hi * 2 + y_lo), z: 8, core: 2. Of those that a mesh axis runs over, the one named last changes fastest.
Arguments:
- panels: bfloat16 [8, 2, 8192, 8192], P('freq', None, 'blk'), parts along dimension 0, may hold values from -30 to 30
- test_matrix: bfloat16 [8192, 256], P('blk'), may hold values from -0.0625 to 0.0625
Outputs:
- projected: float32 [8192, 8, 256], P('blk', 'freq'), parts along dimension 1
There are 4 independent parts, one for each index of `freq`. A program takes and returns all parts, laid end to end along the dimension named above; an argument that names none is the same for every part. Nothing has to cross between parts.
All inputs are finite; a program needn't handle non-finite values.
Results may differ from a plain program's by a relative error of at most 0.0017.
Values may be sent and summed in bfloat16 or wider, within the bound.
A program may use at most 128 MiB of HBM per device.

v0:
```python
import functools

import jax
import jax.numpy as jnp
from jax import lax
from jax.experimental import pallas as pl
from jax.experimental.pallas import tpu as pltpu
from jax.sharding import PartitionSpec as P

F32 = jnp.float32
BF16 = jnp.bfloat16
NX, NY, NZ = 4, 2, 8
X_PIECES = ((0, 0, 256), (1, 0, 32))
Z_PIECES = ((1, 32, 256),)
OFFSETS = (0, 1, 7, 2, 6, 3, 5, 4)
X_GROUPS = ((0, 1), (1, 3), (3, 5), (5, 7), (7, 8))
Y_GROUPS = ((0, 3), (3, 5), (5, 8))
KX = sum(k1 - k0 for _, k0, k1 in X_PIECES)
KZ = sum(k1 - k0 for _, k0, k1 in Z_PIECES)


def scratch():
    dma = pltpu.SemaphoreType.DMA
    buffers = dict(
        om=pltpu.VMEM((NX, NY, NZ, 4, 32, 256), BF16),
        a=pltpu.VMEM((512, 8192), BF16),
        acc=pltpu.VMEM((512, 256), F32),
        st=pltpu.VMEM((2, 256, 256), BF16),
        xs=pltpu.VMEM((2, 2, 8, 2, KX, 128), BF16),
        xr=pltpu.VMEM((2, 2, 8, 2, KX, 128), BF16),
        xacc=pltpu.VMEM((8, 2, KX, 128), F32),
        xys=pltpu.VMEM((8, KX, 128), BF16),
        xy=pltpu.VMEM((8, KX, 128), BF16),
        xzs=pltpu.VMEM((2, 4, KX, 128), F32),
        xzr=pltpu.VMEM((2, 4, KX, 128), F32),
        zs=pltpu.VMEM((2, 4, 4, 2, KZ, 128), BF16),
        zr=pltpu.VMEM((2, 4, 4, 2, KZ, 128), BF16),
        zacc=pltpu.VMEM((4, 2, KZ, 128), F32),
        zy=pltpu.VMEM((4, KZ, 128), F32),
        zxs=pltpu.VMEM((2, 2, KZ, 128), F32),
        zxr=pltpu.VMEM((2, 2, KZ, 128), F32),
        gl=pltpu.VMEM((2, 4, 8, 8, 256), F32),
        gy=pltpu.VMEM((4, 8, 8, 256), F32),
        gx=pltpu.VMEM((3, 8, 8, 256), F32),
        gs=pltpu.VMEM((8, 8, 256), F32),
        gz=pltpu.VMEM((7, 8, 256), F32),
        gf=pltpu.VMEM((4, 8, 8, 256), F32),
        m=pltpu.VMEM((256, 512), F32),
        li=pltpu.VMEM((256, 256), F32),
        pt=pltpu.VMEM((2, 256, 128), F32),
        a_sem=dma,
        oz_s=dma,
        ox_s=dma,
        oy_s=dma,
        ob_s=dma,
        oz_r=dma((NZ,)),
        ox_r=dma((3, 5)),
        oy_r=dma((NX, len(Y_GROUPS))),
        ob_r=dma((2, NX)),
        x_s=dma((2,)),
        x_r=dma((2, 8)),
        xy_s=dma,
        xy_r=dma((8,)),
        xz_s=dma((2,)),
        xz_r=dma((4,)),
        z_s=dma((2,)),
        z_r=dma((4, 4)),
        zy_s=dma,
        zy_r=dma((4,)),
        zx_s=dma((2,)),
        zx_r=dma((2,)),
        gy_s=dma,
        gy_r=dma((4,)),
        gx_s=dma,
        gx_r=dma,
        gz_s=dma,
        gz_r=dma,
        hz_s=dma,
        hz_r=dma,
        hx_s=dma,
        hx_r=dma,
        l_s=dma,
        l_r=dma,
    )
    return list(buffers), list(buffers.values())


NAMES, SHAPES = scratch()


HI = lax.Precision.HIGHEST
PANEL = 32


def factor_group(m, b):
    base = 8 * b
    tile = base // 128
    l0 = base - 128 * tile
    tiles = (0, 1, 2) if tile == 0 else (1, 2, 3)
    end = (base // PANEL + 1) * PANEL
    sub = lax.broadcasted_iota(jnp.int32, (8, 128), 0)

    def full(v):
        return jnp.broadcast_to(v, (8, 128))

    square = m[base:base+8, 128*tile:128*tile+128]
    below = [m[g:g+8, 128*tile:128*tile+128] for g in range(base+8, end, 8)]
    cols = [full(square[:, l0+k:l0+k+1]) for k in range(8)]
    e = [[full(cols[k][i:i+1]) if i >= k else None for k in range(8)] for i in range(8)]
    lower = [[full(g[:, l0+k:l0+k+1]) for k in range(8)] for g in below]
    inv = [None]*8
    for k in range(8):
        inv[k] = lax.rsqrt(e[k][k])
        for i in range(k+1, 8):
            e[i][k] = e[i][k] * inv[k]
        for i in range(k+1, 8):
            for j in range(k+1, i+1):
                e[i][j] = e[i][j] - e[i][k]*e[j][k]
    for g in lower:
        for k in range(8):
            v = g[k]
            for j in range(k):
                v = v - g[j]*e[k][j]
            g[k] = v*inv[k]
    for t in tiles:
        lanes = slice(128*t, 128*t+128)
        rows = m[base:base+8, lanes]
        u = []
        for k in range(8):
            v = full(rows[k:k+1])
            for j in range(k):
                v = v - e[k][j]*u[j]
            u.append(v*inv[k])
        o = u[0]
        for k in range(1, 8):
            o = jnp.where(sub == k, u[k], o)
        m[base:base+8, lanes] = o
        for n, g in enumerate(lower):
            r0 = base+8+8*n
            v = m[r0:r0+8, lanes]
            for k in range(8):
                v = v - g[k]*u[k]
            m[r0:r0+8, lanes] = v

def trailing(m, p):
    end = (p+1)*PANEL
    if end >= 256:
        return
    u0 = m[end-PANEL:end, :]
    for half in (0, 1):
        lo, hi = max(end, 128*half), 128*half+128
        if lo >= hi:
            continue
        first = 128*half
        last = 384 if end <= 128 else 512
        upd = lax.dot_general(u0[:, 128*half:hi], u0[:, first:last], (((0,),(0,)),((),())), precision=HI, preferred_element_type=F32)
        m[lo:hi, first:last] -= upd[lo-128*half:]


class Refs:
    pass


GATHER = (
    ("x", 0, 0), ("x", 0, 1), ("z", 1), ("z", -1), ("z", 2), ("z", -2), ("z", 3), ("z", -3), ("z", 4), ("x", 1, 0),
    ("x", 1, 1), ("y", 0, 0), ("x", 2, 0), ("x", 2, 1), ("y", 0, 1), ("x", 0, 2), ("x", 3, 0), ("x", 3, 1),
    ("x", 1, 2), ("y", 1, 0), ("y", 2, 0), ("x", 4, 0), ("x", 4, 1), ("y", 0, 2), ("s", 0, 0), ("x", 2, 2),
    ("y", 1, 1), ("y", 2, 1), ("x", 3, 2), ("x", 4, 2), ("y", 1, 2), ("s", 1, 0), ("y", 2, 2), ("s", 2, 0),
    ("y", 3, 0), ("y", 3, 1), ("y", 3, 2), ("s", 3, 0), ("k", 0, 0), ("s", 0, 1), ("k", 1, 0), ("s", 1, 1),
    ("k", 2, 0), ("s", 2, 1), ("k", 3, 0), ("k", 0, 1), ("k", 1, 1), ("s", 3, 1), ("k", 2, 1), ("k", 3, 1),
)
SCHEDULE = (
    ("x1", 5), ("z", 0, 2), ("x1", 3), ("z", 0, 1), ("gl",), ("x1", 4), ("z", 0, 0), ("z", 0, 3), ("z", 1, 2),
    ("x1", 1), ("gx", 1), ("gx", 2), ("z", 1, 0), ("z", 1, 3), ("x1", 0), ("gx", 3), ("x2", 3), ("x1", 2),
    ("z", 2, 2), ("gx", 0), ("x2", 1), ("gz",), ("x2", 0), ("z", 1, 1), ("z", 2, 0), ("x2", 2), ("hz",), ("xf", 1),
    ("z", 2, 1), ("z", 3, 2), ("z", 3, 0), ("x1", 6), ("xf", 3), ("hx",), ("xf", 0), ("z", 3, 1), ("xf", 2),
    ("x2", 4), ("zf", 2), ("xz", 0), ("zf", 0), ("x2", 5), ("x2", 6), ("z", 2, 3), ("cs",), ("c", 1), ("zf", 1),
    ("c", 2), ("x1", 7), ("c", 1), ("xz", 1), ("c", 1), ("xf", 4), ("c", 8), ("z", 3, 3), ("c", 2), ("xf", 5),
    ("c", 2), ("zx", 0), ("xz", 2), ("c", 1), ("xf", 6), ("c", 3), ("x2", 7), ("c", 3), ("zf", 3), ("zx", 1),
    ("c", 5), ("xz", 3), ("c", 3), ("xf", 7),
)


def kernel(a_hbm, w_ref, out, *scratch_refs):
    r = Refs()
    for name, ref in zip(NAMES, scratch_refs):
        setattr(r, name, ref)
    me = lax.axis_index("blk")
    fr = lax.axis_index("freq")
    x, y, z, c = me // 16, (me // 8) % 2, me % 8, fr % 2
    d = 1 - 2 * c
    sibling = {"freq": fr + d, "blk": me}

    def at(x_, y_, z_):
        return (((x_ + 8) % 4) * 2 + y_) * 8 + (z_ + 16) % 8

    def to(x_, y_, z_):
        return {"freq": fr, "blk": at(x_, y_, z_)}

    def send(src, dst, send_sem, recv_sem, device):
        pltpu.make_async_remote_copy(
            src_ref=src,
            dst_ref=dst,
            send_sem=send_sem,
            recv_sem=recv_sem,
            device_id=device,
            device_id_type=pl.DeviceIdType.MESH,
        ).start()

    def arrived(sem, ref):
        pltpu.make_async_copy(ref, ref, sem).wait()

    copy_a = pltpu.make_async_copy(a_hbm, r.a, r.a_sem)
    copy_a.start()
    half = pl.ds(2 * c, 2)
    r.om[x, y, 0, half] = w_ref[half]

    barrier = pltpu.get_barrier_semaphore()
    across = {"freq": (fr + 2) % 4, "blk": at(x, 1 - y, z)}
    partners = [to(x + o, y, z) for o in range(1, NX)] + [to(x, y, z + o) for o in range(1, NZ)]
    partners += [to(x, 1 - y, z), across, sibling]
    for partner in partners:
        pl.semaphore_signal(barrier, inc=1, device_id=partner, device_id_type=pl.DeviceIdType.MESH)
    pl.semaphore_wait(barrier, len(partners))

    here = set()

    def need(name, *index):
        if (name, index) in here:
            return
        here.add((name, index))
        if name == "Z":
            arrived(r.oz_r.at[index[0]], r.om.at[x, y, index[0], half])
        elif name == "X":
            k, g = index
            a, b = X_GROUPS[g]
            arrived(r.ox_r.at[k, g], r.om.at[slab_x(1 + k), y, a:b, half])
        elif name == "Y":
            xi, g = index
            a, b = Y_GROUPS[g]
            arrived(r.oy_r.at[xi, g], r.om.at[slab_x(xi), 1 - y, a:b, half])
        else:
            yi, xi = index
            arrived(r.ob_r.at[yi, xi], r.om.at[slab_x(xi), y if yi == 0 else 1 - y, :, half])

    def slab_x(xi):
        return (x + (0, -d, d, 2)[xi] + 4) % 4

    def need_slab(xi, first, last):
        if xi == 0:
            for k in range(max(first, 1), last):
                need("Z", k)
        else:
            for g, (a, b) in enumerate(X_GROUPS):
                if a < last and b > first:
                    need("X", xi - 1, g)

    def z_send(oz):
        k = OFFSETS.index(-oz % NZ)
        send(r.om.at[x, y, 0, half], r.om.at[x, y, k, half], r.oz_s, r.oz_r.at[k], to(x, y, z + oz))

    def z_pass():
        need("Z", 5)
        need("Z", 6)
        send(r.om.at[x, y, 6 - c, half], r.om.at[x, y, 7, half], r.oz_s, r.oz_r.at[7], to(x, y, z + d))

    def x_send(g, k):
        a, b = X_GROUPS[g]
        need_slab(1 if k == 2 else 0, a, b)
        piece = r.om.at[slab_x(1 if k == 2 else 0), y, a:b, half]
        send(piece, piece, r.ox_s, r.ox_r.at[k, g], to(x - d if k == 1 else x + d, y, z))

    def y_send(xi, g):
        a, b = Y_GROUPS[g]
        need_slab(xi, a, b)
        for side, device in enumerate((to(x, 1 - y, z), across)):
            piece = r.om.at[slab_x(xi), y, a:b, 2 * c + side]
            send(piece, piece, r.oy_s, r.oy_r.at[xi, g], device)

    def share(xi, yi):
        if yi == 0:
            need_slab(xi, 0, NZ)
        else:
            for g in range(len(Y_GROUPS)):
                need("Y", xi, g)
        piece = r.om.at[slab_x(xi), y if yi == 0 else 1 - y, :, half]
        send(piece, piece, r.ob_s, r.ob_r.at[yi, (0, 2, 1, 3)[xi]], sibling)

    terms = []

    def sketch(xi, yi):
        if not terms:
            copy_a.wait()
        need("B", yi, xi)
        xx, yy = slab_x(xi), y if yi == 0 else 1 - y
        columns = [r.a[:, pl.ds(pl.multiple_of(at(xx, yy, z + o) * 128, 128), 128)] for o in OFFSETS]
        omega = r.om[xx, yy].reshape(1024, 256)
        value = jnp.dot(jnp.concatenate(columns, axis=1), omega, preferred_element_type=F32)
        r.acc[...] = r.acc[...] + value if terms else value
        terms.append((xi, yi))

    gather = dict(z=z_send, zp=z_pass, x=x_send, y=y_send, s=share, k=sketch)
    for name, *args in GATHER:
        gather[name](*args)

    for s in range(2):
        r.st[s] = r.acc[256 * s : 256 * s + 256].astype(BF16).astype(F32).T.astype(BF16)

    def term(pieces, block, received, out):
        columns = pl.ds(pl.multiple_of(block * 128, 128), 128)
        row = 0
        for s, k0, k1 in pieces:
            n = k1 - k0
            value = jnp.dot(r.st[s, k0:k1, :], r.a[256 * s : 256 * s + 256, columns], preferred_element_type=F32)
            for ref in received:
                value = value + ref[row : row + n, :].astype(F32)
            out[row : row + n, :] = value.astype(out.dtype)
            row += n

    def sg(way):
        return 1 - 2 * way

    def z_off(q):
        return 4 + (q // 2) * (1 - q % 2) - ((q + 1) // 2) * (q % 2)

    def x_off(q):
        return 2 - q + 3 * (q // 2) + 2 * (q // 3)

    def x_send_on(way, s, q):
        if s == 0:
            src, dst = r.xs.at[way, 0, q, way], r.xr.at[way, 0, q, way]
        else:
            src, dst = r.xs.at[way, 1, q], r.xr.at[way, 1, q]
        send(src, dst, r.x_s.at[s], r.x_r.at[s, q], to(x + sg(way), y, z))

    def x1(q):
        for way in (0, 1):
            term(X_PIECES, at(x + 2, way, z + z_off(q)), [], r.xs.at[way, 0, q, way])
            x_send_on(way, 0, q)

    def x2(q):
        arrived(r.x_r.at[0, q], r.xr.at[0, 0, q])
        for way in (0, 1):
            for yy in (0, 1):
                got = [r.xr.at[way, 0, q, way]] if yy == way else []
                term(X_PIECES, at(x + sg(way), yy, z + z_off(q)), got, r.xs.at[way, 1, q, yy])
            x_send_on(way, 1, q)

    def x_fin(q):
        arrived(r.x_r.at[1, q], r.xr.at[:, 1, q])
        for yy in (0, 1):
            got = [r.xr.at[way, 1, q, yy] for way in (0, 1)]
            term(X_PIECES, at(x, yy, z + z_off(q)), got, r.xacc.at[q, yy])
        r.xys[q] = r.xacc[q, 1 - y].astype(BF16)
        send(r.xys.at[q], r.xy.at[q], r.xy_s, r.xy_r.at[q], to(x, 1 - y, z))

    def halves(way, rows):
        return pl.ds(way * (rows // 2), rows // 2)

    def ring_step(total, sent, received, send_sem, recv_sem, s, rows, devices):
        if s:
            ring_arrived(received, recv_sem, s - 1)
        else:
            farthest = total(0)
        for way in (0, 1):
            half_rows = halves(way, rows)
            if s == 0:
                sent[way, 0, half_rows] = farthest[way * (rows // 2) : (way + 1) * (rows // 2)]
                src, dst = sent.at[way, 0, half_rows], received.at[way, 0, half_rows]
            else:
                sent[way, s] = total(2 * s - 1 + way)
                part = half_rows if s == 1 else pl.ds(0, rows)
                sent[way, s, part] += received[way, s - 1, part]
                src, dst = sent.at[way, s], received.at[way, s]
            send(src, dst, send_sem.at[min(s, 1)], recv_sem.at[s], devices[way])

    def ring_arrived(received, recv_sem, s):
        arrived(recv_sem.at[s], received.at[0, 0] if s == 0 else received.at[:, s])

    def x_total(q):
        arrived(r.xy_r.at[q], r.xy.at[q])
        return r.xacc[q, y] + r.xy[q].astype(F32)

    def xz(s):
        ring_step(x_total, r.xzs, r.xzr, r.xz_s, r.xz_r, s, KX, (to(x, y, z + 1), to(x, y, z - 1)))

    def z_arrived(s, q):
        arrived(r.z_r.at[s, q], r.zr.at[0, 0, q] if s == 0 else r.zr.at[:, s, q])

    def z_step(s, q):
        if s:
            z_arrived(s - 1, q)
        for way in (0, 1):
            far = z + sg(way) * (4 - s)
            if s == 0:
                term(Z_PIECES, at(x + x_off(q), way, far), [], r.zs.at[way, 0, q, way])
                src, dst = r.zs.at[way, 0, q, way], r.zr.at[way, 0, q, way]
            else:
                for yy in (0, 1):
                    got = [r.zr.at[way, s - 1, q, yy]] if s > 1 or yy == way else []
                    term(Z_PIECES, at(x + x_off(q), yy, far), got, r.zs.at[way, s, q, yy])
                src, dst = r.zs.at[way, s, q], r.zr.at[way, s, q]
            send(src, dst, r.z_s.at[min(s, 1)], r.z_r.at[s, q], to(x, y, z + sg(way)))

    def z_fin(q):
        z_arrived(3, q)
        for yy in (0, 1):
            got = [r.zr.at[way, 3, q, yy] for way in (0, 1)]
            term(Z_PIECES, at(x + x_off(q), yy, z), got, r.zacc.at[q, yy])
        send(r.zacc.at[q, 1 - y], r.zy.at[q], r.zy_s, r.zy_r.at[q], to(x, 1 - y, z))

    def z_total(q):
        arrived(r.zy_r.at[q], r.zy.at[q])
        return r.zacc[q, y] + r.zy[q]

    def zx(s):
        ring_step(z_total, r.zxs, r.zxr, r.zx_s, r.zx_r, s, KZ, (to(x + 1, y, z), to(x - 1, y, z)))

    def g_local():
        for s in range(2):
            value = jnp.dot(r.st[s], r.acc[256 * s : 256 * s + 256].astype(BF16), preferred_element_type=F32)
            r.gl[s] = value.reshape(4, 8, 8, 256)
        for o in (1, 2, 3, 0):
            k = (x + o) % 4
            send(r.gl.at[1 - y, k], r.gy.at[k], r.gy_s, r.gy_r.at[o], to(x, 1 - y, z))

    def g_x(o):
        k = (x + o) % 4
        arrived(r.gy_r.at[o], r.gy.at[k])
        r.gy[k] += r.gl[y, k]
        if o:
            send(r.gy.at[k], r.gx.at[o - 1], r.gx_s, r.gx_r, to(x + o, y, z))

    def g_z():
        arrived(r.gx_r, r.gx)
        r.gs[...] = r.gy[x] + r.gx[0] + r.gx[1] + r.gx[2]
        for o in range(1, NZ):
            send(r.gs.at[(z + o) % 8], r.gz.at[o - 1], r.gz_s, r.gz_r, to(x, y, z + o))

    def h_z():
        arrived(r.gz_r, r.gz)
        total = r.gs[z]
        for o in range(1, NZ):
            total = total + r.gz[o - 1]
        r.gf[x, z] = total
        piece = r.gf.at[x, z]
        for o in range(1, NZ):
            send(piece, piece, r.hz_s, r.hz_r, to(x, y, z + o))

    def h_x():
        arrived(r.hz_r, r.gf.at[x, 0:7])
        piece = r.gf.at[x]
        for o in range(1, NX):
            send(piece, piece, r.hx_s, r.hx_r, to(x + o, y, z))

    def c_start():
        arrived(r.hx_r, r.gf.at[0:3])
        r.m[:, :256] = r.gf[...].reshape(256, 256)
        row = lax.broadcasted_iota(jnp.int32, (256, 256), 0)
        column = lax.broadcasted_iota(jnp.int32, (256, 256), 1)
        r.m[:, 256:] = jnp.where(row == column, 1.0, 0.0).astype(F32)

    def c_group(b):
        factor_group(r.m, b)
        if (8 * b + 8) % PANEL == 0:
            p = 8 * b // PANEL
            trailing(r.m, p)
            rows = slice(PANEL * p, PANEL * p + PANEL)
            send(r.m.at[rows, 256:512], r.li.at[rows], r.l_s, r.l_r, to(x, 1 - y, z))

    groups = iter(range(32))

    def c_next(n):
        for b in [b for _, b in zip(range(n), groups)]:
            c_group(b)

    steps = dict(
        gl=g_local, z=z_step, x1=x1, x2=x2, gx=g_x, gz=g_z, hz=h_z, hx=h_x, xf=x_fin, zf=z_fin, xz=xz, zx=zx, cs=c_start, c=c_next
    )
    for name, *args in SCHEDULE:
        steps[name](*args)

    for pieces, total, last, received, recv_sem, ring in (
        (Z_PIECES, z_total, 3, r.zxr, r.zx_r, 2),
        (X_PIECES, x_total, 7, r.xzr, r.xz_r, 4),
    ):
        value = total(last)
        ring_arrived(received, recv_sem, ring - 1)
        value = value + received[0, ring - 1] + received[1, ring - 1]
        row = 0
        for s, k0, k1 in pieces:
            n = k1 - k0
            r.pt[s, k0:k1, :] = value[row : row + n]
            row += n

    def solved(s, inverse):
        return lax.dot_general(
            r.pt[s], inverse, (((0,), (1,)), ((), ())), precision=HI, preferred_element_type=F32
        )

    mine = solved(y, r.m[:, 256:])
    arrived(r.l_r, r.li)
    others = solved(1 - y, r.li[...])
    out[:, 0, :] = jnp.where(y == 0, mine, others)
    out[:, 1, :] = jnp.where(y == 0, others, mine)

    for sem, ref in (
        (r.oz_s, r.om.at[x, y, 0:7, half]),
        (r.ox_s, r.om.at[0:3, 0, :, half]),
        (r.oy_s, r.om.at[:, 0, :, half]),
        (r.ob_s, r.om.at[:, :, :, half]),
        (r.x_s.at[0], r.xs.at[0, 0]),
        (r.x_s.at[1], r.xs.at[:, 1]),
        (r.xy_s, r.xys),
        (r.xz_s.at[0], r.xzs.at[0, 0]),
        (r.xz_s.at[1], r.xzs.at[:, 1:4]),
        (r.z_s.at[0], r.zs.at[0, 0]),
        (r.z_s.at[1], r.zs.at[:, 1:4]),
        (r.zy_s, r.zacc.at[:, 0]),
        (r.zx_s.at[0], r.zxs.at[0, 0]),
        (r.zx_s.at[1], r.zxs.at[:, 1]),
        (r.gy_s, r.gl.at[0]),
        (r.gx_s, r.gx),
        (r.gz_s, r.gz),
        (r.hz_s, r.gz),
        (r.hx_s, r.gx),
        (r.l_s, r.li),
    ):
        arrived(sem, ref)


def local(panels, test_matrix):
    return pl.pallas_call(
        kernel,
        out_shape=jax.ShapeDtypeStruct((128, 2, 256), F32),
        in_specs=[pl.BlockSpec(memory_space=pl.ANY), pl.BlockSpec(memory_space=pltpu.VMEM)],
        out_specs=pl.BlockSpec(memory_space=pltpu.VMEM),
        scratch_shapes=SHAPES,
        compiler_params=pltpu.CompilerParams(
            collective_id=0, has_side_effects=True, vmem_limit_bytes=60 * 1024 * 1024
        ),
    )(panels.reshape(512, 8192), test_matrix.reshape(4, 32, 256))


def solution(mesh):
    in_specs = (P("freq", None, "blk", None), P("blk", None))
    out_specs = P("blk", "freq", None)
    return jax.shard_map(local, mesh=mesh, in_specs=in_specs, out_specs=out_specs, check_vma=False)
```

profile of v0, /device:TPU:8, one launch (start us, length us, event | category | flops | bytes accessed | tf_op | source)
XLA Modules:
  0.0 91.5 jit_solution(1113319272154735217)
XLA Ops:
  0.0 89.8 %shard_map.28 = f32[128,2,256]{2,1,0:T(2,128)} custom-call(bf16[512,8192]{1,0:T(8,128)(2,1)} %bitcast.2, bf16[4,32,256]{2,1,0:T(8,128)(2,1)} %bitcast.3), custom_call_target="tpu_custom_call" | custom-call | tf_op jit(solution)/shard_map/pallas_call | solution.py:533
  89.8 1.7 %copy.4 = f32[128,2,256]{2,1,0:T(2,128)} copy(f32[128,2,256]{2,1,0:T(2,128)} %shard_map.28) | data formatting | bytes 524288
where the time goes:
time: 91.7 us; the launch traced here: 91.5 us
  Pallas kernels  89.8 us (98%)
  local copies, waits for them, and re-layouts  1.67 us (2%)
    pallas_call x1, Pallas kernels, local(): pl.pallas_call(kernel, out_shape=jax.ShapeDtypeStruct((128, 2, 256), F32)...  89.8 us

commit v1 on v0

--- a/solution.py
+++ b/solution.py
@@ -170,14 +170,14 @@
     ("k", 2, 0), ("s", 2, 1), ("k", 3, 0), ("k", 0, 1), ("k", 1, 1), ("s", 3, 1), ("k", 2, 1), ("k", 3, 1),
 )
 SCHEDULE = (
-    ("x1", 5), ("z", 0, 2), ("x1", 3), ("z", 0, 1), ("gl",), ("x1", 4), ("z", 0, 0), ("z", 0, 3), ("z", 1, 2),
-    ("x1", 1), ("gx", 1), ("gx", 2), ("z", 1, 0), ("z", 1, 3), ("x1", 0), ("gx", 3), ("x2", 3), ("x1", 2),
-    ("z", 2, 2), ("gx", 0), ("x2", 1), ("gz",), ("x2", 0), ("z", 1, 1), ("z", 2, 0), ("x2", 2), ("hz",), ("xf", 1),
-    ("z", 2, 1), ("z", 3, 2), ("z", 3, 0), ("x1", 6), ("xf", 3), ("hx",), ("xf", 0), ("z", 3, 1), ("xf", 2),
-    ("x2", 4), ("zf", 2), ("xz", 0), ("zf", 0), ("x2", 5), ("x2", 6), ("z", 2, 3), ("cs",), ("c", 1), ("zf", 1),
-    ("c", 2), ("x1", 7), ("c", 1), ("xz", 1), ("c", 1), ("xf", 4), ("c", 8), ("z", 3, 3), ("c", 2), ("xf", 5),
-    ("c", 2), ("zx", 0), ("xz", 2), ("c", 1), ("xf", 6), ("c", 3), ("x2", 7), ("c", 3), ("zf", 3), ("zx", 1),
-    ("c", 5), ("xz", 3), ("c", 3), ("xf", 7),
+    ("x1", 1), ("z", 0, 1), ("x1", 3), ("z", 0, 2), ("gl",), ("z", 0, 3), ("z", 0, 0), ("x1", 2), ("x1", 6),
+    ("z", 1, 1), ("z", 1, 2), ("gx", 1), ("gx", 2), ("gx", 3), ("x1", 0), ("z", 1, 0), ("x2", 1), ("z", 2, 1),
+    ("gx", 0), ("gz",), ("x2", 0), ("x2", 2), ("z", 2, 0), ("z", 2, 2), ("x1", 4), ("x2", 3), ("xf", 0), ("hz",),
+    ("z", 3, 0), ("z", 3, 1), ("z", 1, 3), ("z", 3, 2), ("xz", 0), ("x1", 5), ("xf", 2), ("xf", 1), ("hx",),
+    ("zf", 0), ("x2", 4), ("x2", 5), ("x2", 6), ("xf", 3), ("zf", 1), ("x1", 7), ("zx", 0), ("z", 2, 3), ("cs",),
+    ("zf", 2), ("c", 4), ("xz", 1), ("c", 2), ("xf", 4), ("c", 7), ("z", 3, 3), ("xf", 5), ("c", 5), ("xz", 2),
+    ("c", 1), ("xf", 6), ("c", 3), ("x2", 7), ("c", 1), ("zf", 3), ("c", 1), ("zx", 1), ("c", 5), ("xz", 3), ("c", 3),
+    ("xf", 7),
 )
 
 

time: 91.7 us -> 90.3 us (0.985)
  Pallas kernels: 89.8 us -> 88.5 us
    pallas_call x1, Pallas kernels: 89.8 us -> 88.5 us  [local(): pl.pallas_call(kernel, out_shape=jax.ShapeDtypeStruct((128, 2, 256), F32)...]
where the time goes in v1:
time: 90.3 us; the launch traced here: 90.2 us
  Pallas kernels  88.5 us (98%)
  local copies, waits for them, and re-layouts  1.67 us (2%)
    pallas_call x1, Pallas kernels, local(): pl.pallas_call(kernel, out_shape=jax.ShapeDtypeStruct((128, 2, 256), F32)...  88.5 us

profile of v1, /device:TPU:8, one launch (start us, length us, event | category | flops | bytes accessed | tf_op | source)
XLA Modules:
  0.0 90.2 jit_solution(15610813210807336023)
XLA Ops:
  0.0 88.5 %shard_map.28 = f32[128,2,256]{2,1,0:T(2,128)} custom-call(bf16[512,8192]{1,0:T(8,128)(2,1)} %bitcast.2, bf16[4,32,256]{2,1,0:T(8,128)(2,1)} %bitcast.3), custom_call_target="tpu_custom_call" | custom-call | tf_op jit(solution)/shard_map/pallas_call | solution.py:533
  88.5 1.7 %copy.4 = f32[128,2,256]{2,1,0:T(2,128)} copy(f32[128,2,256]{2,1,0:T(2,128)} %shard_map.28) | data formatting | bytes 524288
